TPU v7x, 128 devices: a whole 4x4x4 slice. The times are simulated.
128 devices in a mesh: row: 4 (over y_hi, core), col: 32 (over z, y_lo, x).
Axes of the slice: x: 4, y: 4 (y_hi: 2, y_lo: 2; y = y_hi * 2 + y_lo), z: 4, core: 2. Of those that a mesh axis runs over, the one named last changes fastest.
Arguments:
- pair_amps: float32 [640, 25600], P('row', 'col'), may hold values from -6 to 6
- cycle_w: float32 [25600, 25600], P('row', 'col'), may hold values from -0.0390625 to 0.0390625
Outputs:
- cycle_term: float32 [640, 25600], P('row', 'col')
All inputs are finite; a program needn't handle non-finite values.
Results may differ from a plain program's by a relative error of at most 0.00007.
Values sent between devices are 32-bit elements; how exact they have to be, the bound alone decides.
No kernel may reach another device: no remote copies, remote signals or barrier semaphores. Data moves between devices by JAX's collectives and lax.ppermute only.
A program may use at most 192 MiB of HBM per device.

v0:
```python
import jax
import jax.numpy as jnp
from jax import lax
from jax.sharding import PartitionSpec as P

O = 40
A_SLAB = 16


def to_panel(block):
    virt_count = block.shape[0]
    return (
        block.reshape(virt_count, O, O, A_SLAB)
        .transpose(3, 1, 0, 2)
        .reshape(A_SLAB * O, virt_count * O)
    )


def per_device(pair_amps, cycle_w):
    regrouped = to_panel(lax.all_to_all(pair_amps, "col", split_axis=0, concat_axis=1, tiled=True))
    whole_panel = lax.all_gather(regrouped, "col", axis=1, tiled=True)
    return lax.psum_scatter(
        jnp.dot(
            whole_panel,
            cycle_w,
            precision=lax.Precision.HIGHEST,
            preferred_element_type=jnp.float32,
        ),
        "row",
        scatter_dimension=0,
        tiled=True,
    )


def solution(mesh):
    return jax.shard_map(
        per_device,
        mesh=mesh,
        in_specs=(P("row", "col"), P("row", "col")),
        out_specs=P("row", "col"),
        check_vma=False,
    )
```

profile of v0, /device:TPU:1, one launch (start us, length us, event | category | flops | bytes accessed | tf_op | source)
XLA Modules:
  0.0 383.4 jit_solution(15113171651141956955)
XLA Ops:
  6.5 0.0 all-gather.2.cloned.1.call-start
  6.5 1.1 all_to_all.12
  7.7 23.5 %all_to_all.16 = f32[32,5,800]{2,1,0:T(8,128)S(1)} all-to-all(f32[32,5,800]{2,1,0:T(8,128)S(1)} %all_to_all.12), channel_id=1, replica_groups=mesh['row'=4,'col'=32] {'col'}, dimensions={0} | all-to-all | bytes 1024000 | tf_op jit(solution)/shard_map/all_to_all | solution.py:20
  31.2 0.1 copy.3
  31.3 2.9 reshape.10
  34.3 3.9 %copy.4 = f32[16,40,5,40]{1,0,3,2:T(8,128)S(1)} copy(f32[16,40,5,40]{0,3,1,2:T(8,128)} %bitcast.8) | data formatting | bytes 1024000 | tf_op jit(solution)/shard_map/transpose | solution.py:14
  38.2 1.6 reshape.11
  39.7 0.0 all-gather.2.cloned.1.call-update
  39.7 0.0 reduce-scatter.2.cloned.1.call-start
  39.8 180.6 %all-gather.2.cloned.1.call-done = f32[640,6400]{0,1:T(8,128)} async-done(((f32[640,200]{0,1:T(8,128)}), f32[640,6400]{0,1:T(8,128)}) %all-gather.2.cloned.1.call-update) | async-done | bytes 16384016 | tf_op jit(solution)/shard_map/all_gather | solution.py:21
  220.4 106.7 %fusion = f32[640,800]{1,0:T(8,128)} fusion(f32[640,6400]{0,1:T(8,128)} %all-gather.2.cloned.1.call-done, f32[6400,800]{0,1:T(8,128)} %param.3), kind=kOutput, calls=%fused_computation | convolution fusion | flops 39321600000 | bytes 38912000 | tf_op jit(solution)/shard_map/dot_general | solution.py:23
  327.1 0.0 reduce-scatter.2.cloned.1.call-update
  327.2 49.3 %reduce-scatter.2.cloned.1.call-done = f32[160,800]{1,0:T(8,128)} async-done(((f32[640,800]{1,0:T(8,128)}), f32[160,800]{1,0:T(8,128)}) %reduce-scatter.2.cloned.1.call-update) | async-done | bytes 512016 | tf_op jit(solution)/shard_map/reduce_scatter | solution.py:22
Async XLA Ops:
  6.5 213.9 %all-gather.2.cloned.1.call-start = ((), (), s32[]{:S(2)}) async-start(), calls=%async_computation.2 | async-start | bytes 16896000 | tf_op jit(solution)/shard_map/all_gather | solution.py:21
  39.7 336.8 %reduce-scatter.2.cloned.1.call-start = ((), (), s32[]{:S(2)}) async-start(), calls=%async_computation.3 | async-start | bytes 2867200 | tf_op jit(solution)/shard_map/reduce_scatter | solution.py:22
Sparse Core Ops, SparseCore 0:
  39.9 180.5 all-gather.1
  327.3 49.1 reduce-scatter.1
where the time goes:
time: 384 us; the launch traced here: 383 us
  waiting for transfers between devices  230 us (60%)
  matrix products  107 us (28%)
  blocking collectives  23.5 us (6%)
  between operations  13.4 us (3%)
  local copies, waits for them, and re-layouts  9.61 us (3%)
    all_gather x1, waiting for transfers between devices, per_device(): whole_panel = lax.all_gather(regrouped, 'col', axis=1, tiled=True)  181 us
    dot_general x1, matrix products, per_device(): jnp.dot(whole_panel, cycle_w, precision=lax.Precision.HIGHEST, preferred_...  107 us
    reduce_scatter x1, waiting for transfers between devices, per_device(): lax.psum_scatter(jnp.dot(whole_panel, cycle_w, precision=lax.Precision.HI...  49.3 us
    all_to_all x1, blocking collectives, per_device(): lax.all_to_all(pair_amps, 'col', split_axis=0, concat_axis=1, tiled=True)  23.5 us
  transfers between devices with their start and end apart: 2, of which 2 were waited for; matrix products, arithmetic and copies ran while one was open for 0% of the time, Pallas kernels for 0%

commit v1 on v0

v1 whole, which is shorter than its diff:
```python
import functools

import jax
import jax.numpy as jnp
from jax import lax
from jax.experimental import pallas as pl
from jax.experimental.pallas import tpu as pltpu
from jax.sharding import PartitionSpec as P

O = 40
PAY = 63
KMAIN, KTAIL = 5120, 1280
KBLK = 1280
VLIM = 56 * 1024 * 1024


def pack_kernel(sc_ref, p_ref, o0_ref, o1_ref, main, tail):
    base = pl.multiple_of(sc_ref[0] * 32, 32)
    tail[...] = jnp.zeros_like(tail)
    for k in range(7):
        if k < 6:
            x = p_ref[:, 128 * k : 128 * k + 128]
            rows = 128
        else:
            x = jnp.concatenate([p_ref[:, 768:800], jnp.zeros((160, 96), jnp.float32)], axis=1)
            rows = 32
        x = jnp.concatenate([x, jnp.zeros((96, 128), jnp.float32)], axis=0)
        xt = x.T
        main[128 * k : 128 * k + rows, :] = xt[:rows, :128]
        tail[pl.ds(base + 128 * k, rows), :] = xt[:rows, 128:]
    for h, o_ref in ((0, o0_ref), (1, o1_ref)):
        for s in range(8):
            a = 4 * (s // 2) + 2 * h + s % 2
            o_ref[pl.ds(s, 50, stride=8), :] = main[pl.ds(a, 50, stride=16), :]
            t = tail[pl.ds(a, 13, stride=64), :]
            for q in range(1, 4):
                t = t + pltpu.roll(tail[pl.ds(16 * q + a, 13, stride=64), :], 32 * q, 1)
            o_ref[pl.ds(400 + s, 13, stride=8), :] = t


def pack(scal, p):
    full = pl.BlockSpec(memory_space=pltpu.VMEM)
    return pl.pallas_call(
        pack_kernel,
        out_shape=[jax.ShapeDtypeStruct((PAY * 8, 128), jnp.float32)] * 2,
        in_specs=[pl.BlockSpec(memory_space=pltpu.SMEM), full],
        out_specs=[full, full],
        scratch_shapes=[pltpu.VMEM((800, 128), jnp.float32), pltpu.VMEM((832, 128), jnp.float32)],
        compiler_params=pltpu.CompilerParams(vmem_limit_bytes=VLIM),
        cost_estimate=pl.CostEstimate(flops=0, bytes_accessed=1_000_000, transcendentals=0),
        name="pack",
    )(scal, p)


def split_kernel(w_ref, h_ref, l_ref):
    n = pl.program_id(0)

    def body(j, last):
        x = w_ref[pl.ds(j, 160, stride=O), :]
        if last:
            lane = lax.broadcasted_iota(jnp.int32, x.shape, 1)
            x = jnp.where(lane < 32, x, 0.0)
        hi = x.astype(jnp.bfloat16)
        res = x - hi.astype(jnp.float32)
        m = pl.ds(pl.multiple_of(j * 128, 128), 128)
        t = pl.ds(pl.multiple_of(KMAIN + j * 32, 32), 32)
        if last:
            both = (hi.astype(jnp.float32) + pltpu.roll(res, 32, 1)).astype(jnp.bfloat16)
            h_ref[m, :] = both[:128]
            h_ref[t, :] = both[128:]
        else:
            lo = res.astype(jnp.bfloat16)
            h_ref[m, :] = hi[:128]
            h_ref[t, :] = hi[128:]
            l_ref[m, :] = lo[:128]
            l_ref[t, :] = lo[128:]

    @pl.when(n < 6)
    def _():
        pl.loop(0, O, unroll=2)(functools.partial(body, last=False))

    @pl.when(n == 6)
    def _():
        pl.loop(0, O, unroll=2)(functools.partial(body, last=True))


def split_weights(w):
    return pl.pallas_call(
        split_kernel,
        grid=(7,),
        out_shape=[
            jax.ShapeDtypeStruct((6400, 896), jnp.bfloat16),
            jax.ShapeDtypeStruct((6400, 768), jnp.bfloat16),
        ],
        in_specs=[pl.BlockSpec((6400, 128), lambda n: (0, n))],
        out_specs=[
            pl.BlockSpec((6400, 128), lambda n: (0, n)),
            pl.BlockSpec((6400, 128), lambda n: (0, jnp.minimum(n, 5))),
        ],
        compiler_params=pltpu.CompilerParams(vmem_limit_bytes=VLIM),
        cost_estimate=pl.CostEstimate(flops=20_000_000, bytes_accessed=44_000_000, transcendentals=0),
        name="split_w",
    )(w)


def product_kernel(places, slots, sc_ref, *refs):
    n_in = len(places)
    ins, (h_ref, l_ref), outs = refs[:n_in], refs[n_in : n_in + 2], refs[n_in + 2 : n_in + 6]
    a_s, t_s, lhs, hb, lb, acc1, acc2, zs, asem, wsem = refs[n_in + 6 :]
    x0, r0 = sc_ref[1], sc_ref[2]
    rows = 40 * slots
    mp = lhs.shape[0] // 2

    def wcopy(kb, buf):
        src = pl.ds(pl.multiple_of(kb * KBLK, KBLK), KBLK)
        return (
            pltpu.make_async_copy(h_ref.at[src], hb.at[buf], wsem.at[buf, 0]),
            pltpu.make_async_copy(l_ref.at[src], lb.at[buf], wsem.at[buf, 1]),
        )

    copies = []
    for op, where in zip(ins, places):
        for at, (slot, dx) in enumerate(where):
            x = lax.rem(x0 + dx, 4)
            copies.append(pltpu.make_async_copy(op.at[at, pl.ds(0, 50)], a_s.at[slot, pl.ds(50 * x, 50)], asem.at[0]))
            copies.append(pltpu.make_async_copy(op.at[at, pl.ds(50, 13)], t_s.at[slot, x], asem.at[1]))
    for c in copies:
        c.start()
    for c in wcopy(0, 0):
        c.start()
    for c in copies:
        c.wait()

    def put(at, parts):
        v = jnp.concatenate(parts, axis=0)
        if mp > rows:
            v = jnp.concatenate([v, jnp.zeros((mp - rows, 128), jnp.float32)], axis=0)
        hi = v.astype(jnp.bfloat16)
        lhs[0:mp, at * 128 : at * 128 + 128] = hi
        lhs[mp:, at * 128 : at * 128 + 128] = (v - hi.astype(jnp.float32)).astype(jnp.bfloat16)

    def block(kb, buf, first):
        for c in wcopy(kb, buf):
            c.wait()
        left = lhs[...]
        p1 = jnp.dot(left, hb[buf], preferred_element_type=jnp.float32)
        p2 = jnp.dot(left[:mp], lb[buf], preferred_element_type=jnp.float32)
        if first:
            acc1[...] = p1
            acc2[...] = p2
        else:
            acc1[...] += p1
            acc2[...] += p2

    acc1[...] = jnp.zeros_like(acc1)
    acc2[...] = jnp.zeros_like(acc2)

    @pl.loop(0, 4)
    def _(kb):
        buf = lax.rem(kb, 2)
        for c in wcopy(kb + 1, 1 - buf):
            c.start()
        for jj in range(10):
            j = kb * 10 + jj
            put(jj, [a_s[s, 40 * i + j] for s in range(slots) for i in range(5)])
        block(kb, buf, False)

    def tail_tile(s, t):
        if t == 12:
            return t_s[s, 0, 12] + t_s[s, 1, 0]
        if t == 37:
            return t_s[s, 2, 12] + t_s[s, 3, 0]
        if t < 12:
            return t_s[s, 0, t]
        if t < 25:
            return t_s[s, 1, t - 12]
        if t < 37:
            return t_s[s, 2, t - 25]
        return t_s[s, 3, t - 37]

    for g in range(10):
        put(g, [tail_tile(s, 10 * i + g) for s in range(slots) for i in range(5)])
    block(4, 0, False)

    n5 = 5 * slots
    for n in range(7):
        lanes = slice(128 * n, 128 * n + 128)
        z = acc1[0:rows, lanes] + acc1[mp : mp + rows, lanes]
        if n < 6:
            z = z + acc2[0:rows, lanes]
        else:
            z = z + pltpu.roll(acc1[0:rows, lanes], 96, 1)
        zs[n] = z
    for k, out in enumerate(outs):
        to = jnp.bitwise_xor(r0, k)
        for e in range(2):
            for n in range(7):
                wide = 128 if n < 6 else 32
                v = zs[n, pl.ds(2 * to + e, n5, stride=8), :]
                out[e * n5 : e * n5 + n5, 128 * n : 128 * n + wide] = v[:, :wide]


def product(scal, operands, places, slots, h, l):
    mp = -(-40 * slots // 16) * 16
    anyspec = pl.BlockSpec(memory_space=pl.ANY)
    f32, bf16 = jnp.float32, jnp.bfloat16
    return pl.pallas_call(
        functools.partial(product_kernel, places, slots),
        out_shape=[jax.ShapeDtypeStruct((10 * slots, 800), f32)] * 4,
        in_specs=[pl.BlockSpec(memory_space=pltpu.SMEM)] + [anyspec] * (len(operands) + 2),
        out_specs=[pl.BlockSpec(memory_space=pltpu.VMEM)] * 4,
        scratch_shapes=[
            pltpu.VMEM((slots, 200, 8, 128), f32),
            pltpu.VMEM((slots, 4, 13, 8, 128), f32),
            pltpu.VMEM((2 * mp, KBLK), bf16),
            pltpu.VMEM((2, KBLK, 896), bf16),
            pltpu.VMEM((2, KBLK, 768), bf16),
            pltpu.VMEM((2 * mp, 896), f32),
            pltpu.VMEM((mp, 768), f32),
            pltpu.VMEM((7, 40 * slots, 128), f32),
            pltpu.SemaphoreType.DMA((2,)),
            pltpu.SemaphoreType.DMA((2, 2)),
        ],
        compiler_params=pltpu.CompilerParams(vmem_limit_bytes=VLIM),
        cost_estimate=pl.CostEstimate(flops=40 * slots * 6400 * 800 * 6, bytes_accessed=22_000_000, transcendentals=0),
        name="product",
    )(scal, *operands, h, l)


def place_kernel(chunks, sc_ref, *refs):
    o_ref, o_s = refs[-2], refs[-1]
    z0, y0 = sc_ref[3], sc_ref[4]
    for c, slots in enumerate(chunks):
        n5 = 5 * len(slots)
        a, b, d, e = (refs[4 * c + k][...] for k in range(4))
        v = (a + b) + (d + e)
        for half_e in range(2):
            for s, (h, dz, dy) in enumerate(slots):
                g = 2 * lax.rem(z0 + dz, 4) + lax.rem(y0 + dy, 2)
                at = half_e * n5 + 5 * s
                o_s[2 * h + half_e, g, 0:5, :] = v[at : at + 5, :]
    for a2 in range(4):
        for g in range(8):
            o_ref[40 * a2 + 5 * g : 40 * a2 + 5 * g + 5, :] = o_s[a2, g, 0:5, :]


def place(scal, chunks, arrays):
    full = pl.BlockSpec(memory_space=pltpu.VMEM)
    return pl.pallas_call(
        functools.partial(place_kernel, chunks),
        out_shape=jax.ShapeDtypeStruct((160, 800), jnp.float32),
        in_specs=[pl.BlockSpec(memory_space=pltpu.SMEM)] + [full] * len(arrays),
        out_specs=full,
        scratch_shapes=[pltpu.VMEM((4, 8, 8, 800), jnp.float32)],
        compiler_params=pltpu.CompilerParams(vmem_limit_bytes=VLIM),
        cost_estimate=pl.CostEstimate(flops=1_000_000, bytes_accessed=3_000_000, transcendentals=0),
        name="place",
    )(scal, *arrays)


def cidx(z, y, x):
    return (z % 4) * 8 + (y % 2) * 4 + x % 4


def shift(dz=0, dy=0, dx=0):
    return [(cidx(z, y, x), cidx(z + dz, y + dy, x + dx)) for z in range(4) for y in range(2) for x in range(4)]


XP, XM, ZP, ZM, YY = shift(dx=1), shift(dx=-1), shift(dz=1), shift(dz=-1), shift(dy=1)


def send(v, perm):
    return lax.ppermute(v, "col", perm)


def after(v, *others):
    return lax.optimization_barrier((v, *others))[0]


def to_peers(outs):
    return [outs[0]] + [lax.ppermute(outs[k], "row", [(r, r ^ k) for r in range(4)]) for k in (1, 2, 3)]


def per_device(pair_amps, cycle_w):
    c, r = lax.axis_index("col"), lax.axis_index("row")
    x0, y0, z0 = c % 4, (c // 4) % 2, c // 8
    scal = jnp.stack([c % 2, x0, r, z0, y0]).astype(jnp.int32)
    pay0, pay1 = pack(scal, pair_amps)
    pay0, pay1 = pay0.reshape(1, PAY, 8, 128), pay1.reshape(1, PAY, 8, 128)

    fm0, fp0 = send(pay0, XP), send(pay0, XM)
    fm1, fp1 = send(pay1, ZP), send(pay1, ZM)
    w0 = jnp.concatenate([send(fm0[:, :32], XP), send(fp0[:, 32:], XM)], axis=1)
    w1 = jnp.concatenate([send(fm1[:, :32], ZP), send(fp1[:, 32:], ZM)], axis=1)
    g0 = jnp.concatenate([pay0, fm0, fp0, w0], axis=0)
    c1 = jnp.concatenate([pay1, fm1], axis=0), jnp.concatenate([fp1, w1], axis=0)
    g1 = jnp.concatenate([*c1], axis=0)

    y1a = send(c1[0], YY)
    y0g = send(after(g0, y1a), YY)
    y1b = send(after(c1[1], y0g), YY)

    zm, zp = send(g0, ZP), send(g0, ZM)
    xm, xp = send(g1, XP), send(g1, XM)
    wl = after(cycle_w, g0, g1)
    wh, wlo = split_weights(wl)
    zf, zb = send(zm[:2], ZP), send(zp[2:], ZM)
    xf, xb = send(xm[:2], XP), send(xp[2:], XM)

    yzm, yzp = send(after(y0g, zf), ZP), send(after(y0g, zb), ZM)
    yxm0, yxp0 = send(after(y1a, xf), XP), send(after(y1a, xb), XM)
    yxm1, yxp1 = send(after(y1b, yxm0), XP), send(after(y1b, yxp0), XM)
    yzf, yzb = send(yzm[:2], ZP), send(yzp[2:], ZM)
    yxf, yxb = send(after(yxm0, yxm1), XP), send(yxp1, XM)

    dxs = (0, 3, 1, 2)
    row = lambda s: [(s, d) for d in dxs]
    col = lambda d, n=4, s0=0: [(s0 + s, d) for s in range(n)]

    oa = product(scal, [g0, zm, zp, zf, zb, y0g], [row(0), row(1), row(2), row(3)[:2], row(3)[2:], row(4)], 5, wh, wlo)
    sa = [(0, 0, 0), (0, 3, 0), (0, 1, 0), (0, 2, 0), (0, 0, 1)]
    ob = product(scal, [g1, xm, xp, xf, xb], [col(0), col(3), col(1), col(2, 2), col(2, 2, 2)], 4, wh, wlo)
    sb = [(1, 0, 0), (1, 3, 0), (1, 1, 0), (1, 2, 0)]
    oc = product(scal, [yzm, yzp], [row(0), row(1)], 2, wh, wlo)
    sc = [(0, 3, 1), (0, 1, 1)]
    od = product(
        scal,
        [yzf, yzb, y1a, y1b, yxm0, yxm1, yxp0, yxp1, yxf, yxb],
        [row(0)[:2], row(0)[2:], col(0, 2, 1), col(0, 2, 3), col(3, 2, 1), col(3, 2, 3), col(1, 2, 1), col(1, 2, 3), col(2, 2, 1), col(2, 2, 3)],
        5,
        wh,
        wlo,
    )
    sd = [(0, 2, 1), (1, 0, 1), (1, 3, 1), (1, 1, 1), (1, 2, 1)]
    return place(scal, (sa, sb, sc, sd), [v for o in (oa, ob, oc, od) for v in to_peers(o)])


def solution(mesh):
    return jax.shard_map(
        per_device,
        mesh=mesh,
        in_specs=(P("row", "col"), P("row", "col")),
        out_specs=P("row", "col"),
        check_vma=False,
    )
```

time: 384 us -> 211 us (0.55)
  waiting for transfers between devices: 230 us -> 32.6 us
  matrix products: 107 us -> 0 us
  Pallas kernels: 0 us -> 82.6 us
  starting transfers between devices: 0.04 us -> 63.3 us
  blocking collectives: 23.5 us -> 0 us
  local copies, waits for them, and re-layouts: 9.61 us -> 28.1 us
  between operations: 13.4 us -> 0.62 us
    all_gather x1 -> x0, waiting for transfers between devices: 181 us -> none  [per_device(): whole_panel = lax.all_gather(regrouped, 'col', axis=1, tiled=True)]
    dot_general x1 -> x0, matrix products: 107 us -> none  [per_device(): jnp.dot(whole_panel, cycle_w, precision=lax.Precision.HIGHEST, preferred_...]
    pallas_call x0 -> x7, Pallas kernels: none -> 82.6 us  [the longest x4 56.3 us: product(): pl.pallas_call(functools.partial(product_kernel, places, slots), out_shap...]
    ppermute x0 -> x41, starting transfers between devices: none -> 63.3 us  [the longest x29 40.5 us: send(): return lax.ppermute(v, 'col', perm)]
    reduce_scatter x1 -> x0, waiting for transfers between devices: 49.3 us -> none  [per_device(): lax.psum_scatter(jnp.dot(whole_panel, cycle_w, precision=lax.Precision.HI...]
    ppermute x0 -> x41, waiting for transfers between devices: none -> 32.6 us  [the longest x29 27.1 us: send(): return lax.ppermute(v, 'col', perm)]
    all_to_all x1 -> x0, blocking collectives: 23.5 us -> none  [per_device(): lax.all_to_all(pair_amps, 'col', split_axis=0, concat_axis=1, tiled=True)]
    optimization_barrier x0 -> x1, local copies, waits for them, and re-layouts: none -> 23.5 us  [after(): return lax.optimization_barrier((v, *others))[0]]
  transfers between devices with their start and end apart: 2 -> 41, of which waited for: 2 -> 10; matrix products, arithmetic and copies ran while one was open for 0% -> 13% of each run, Pallas kernels for 0% -> 37%
where the time goes in v1:
time: 211 us; the launch traced here: 210 us
  Pallas kernels  82.6 us (39%)
  starting transfers between devices  63.3 us (30%)
  waiting for transfers between devices  32.6 us (15%)
  local copies, waits for them, and re-layouts  28.1 us (13%)
  other arithmetic  3.13 us (1%)
    pallas_call x4, Pallas kernels, product(): pl.pallas_call(functools.partial(product_kernel, places, slots), out_shap...  56.3 us
    ppermute x29, starting transfers between devices, send(): return lax.ppermute(v, 'col', perm)  40.5 us
    ppermute x29, waiting for transfers between devices, send(): return lax.ppermute(v, 'col', perm)  27.1 us
    optimization_barrier x1, local copies, waits for them, and re-layouts, after(): return lax.optimization_barrier((v, *others))[0]  23.5 us
    ppermute x12, starting transfers between devices, to_peers(): lax.ppermute(outs[k], 'row', [(r, r ^ k) for r in range(4)])  22.7 us
    pallas_call x1, Pallas kernels, split_weights(): pl.pallas_call(split_kernel, grid=(7,), out_shape=[jax.ShapeDtypeStruct((...  21 us
    ppermute x12, waiting for transfers between devices, to_peers(): lax.ppermute(outs[k], 'row', [(r, r ^ k) for r in range(4)])  5.43 us
  transfers between devices with their start and end apart: 41, of which 10 were waited for; matrix products, arithmetic and copies ran while one was open for 13% of the time, Pallas kernels for 37%

profile of v1, /device:TPU:1, one launch (start us, length us, event | category | flops | bytes accessed | tf_op | source)
XLA Modules:
  0.0 210.3 jit_solution(4887014862464291801)
XLA Ops:
  0.0 0.7 stack.23.sc_ref
  0.7 2.4 %pack.1 = (f32[504,128]{1,0:T(8,128)}, f32[504,128]{1,0:T(8,128)}) custom-call(s32[5]{0:T(128)} %stack.23.sc_ref, f32[160,800]{1,0:T(8,128)} %p_ref.1), custom_call_target="tpu_custom_call" | custom-call | bytes 1000000 | tf_op jit(solution)/shard_map/pack/pallas_call | solution.py:43
  3.1 2.5 %collective-permute-start.8 = (f32[1,63,8,128]{3,2,1,0:T(8,128)}, f32[1,63,8,128]{3,2,1,0:T(8,128)S(1)}, u32[]{:S(2)}, u32[]{:S(2)}) collective-permute-start(f32[1,63,8,128]{3,2,1,0:T(8,128)} %bitcast.7), channel_id=1, source_target_pairs={{0,8},{1,9},{2,10},{3,11},{4,12},{5,13},{6,14},{7,15},{8,16},{9,17... | collective-permute-start | bytes 774152 | tf_op jit(solution)/shard_map/ppermute | solution.py:273
  5.6 2.1 %collective-permute-start.11 = (f32[1,63,8,128]{3,2,1,0:T(8,128)}, f32[1,63,8,128]{3,2,1,0:T(8,128)S(1)}, u32[]{:S(2)}, u32[]{:S(2)}) collective-permute-start(f32[1,63,8,128]{3,2,1,0:T(8,128)} %bitcast.8), channel_id=1, source_target_pairs={{0,24},{1,25},{2,26},{3,27},{4,28},{5,29},{6,30},{7,31},{8,0},{9,1... | collective-permute-start | bytes 774152 | tf_op jit(solution)/shard_map/ppermute | solution.py:273
  7.7 1.2 collective-permute-start
  8.9 1.5 collective-permute-start.1
  10.4 3.5 %collective-permute-done.8 = f32[1,63,8,128]{3,2,1,0:T(8,128)S(1)} collective-permute-done((f32[1,63,8,128]{3,2,1,0:T(8,128)}, f32[1,63,8,128]{3,2,1,0:T(8,128)S(1)}, u32[]{:S(2)}, u32[]{:S(2)}) %collective-permute-start.8) | collective-permute-done | bytes 258080 | tf_op jit(solution)/shard_map/ppermute | solution.py:273
  13.9 0.1 collective-permute-start.12
  14.0 2.7 %collective-permute-start.13 = (f32[1,31,8,128]{3,2,1,0:T(8,128)S(1)}, f32[1,31,8,128]{3,2,1,0:T(8,128)S(1)}, u32[]{:S(2)}, u32[]{:S(2)}) collective-permute-start(f32[1,31,8,128]{3,2,1,0:T(8,128)S(1)} %slice.45), channel_id=1, source_target_pairs={{0,24},{1,25},{2,26},{3,27},{4,28},{5,29},{6,30},{7,31},{8,0},{9,1... | collective-permute-start | bytes 380936 | tf_op jit(solution)/shard_map/ppermute | solution.py:273
  16.7 1.3 collective-permute-start.2
  18.0 1.5 collective-permute-start.3
  19.5 1.0 pad_maximum_fusion.1
  20.5 1.4 collective-permute-start.9
  21.9 1.1 pad_maximum_fusion.refs_0_
  23.0 0.1 collective-permute-start.17
  23.1 2.7 %collective-permute-start.18 = (f32[4,63,8,128]{3,2,1,0:T(8,128)S(1)}, f32[4,63,8,128]{3,2,1,0:T(8,128)S(1)}, u32[]{:S(2)}, u32[]{:S(2)}) collective-permute-start(f32[4,63,8,128]{3,2,1,0:T(8,128)S(1)} %pad_maximum_fusion.refs_0_), channel_id=1, source_target_pairs={{0,3},{1,0},{2,1},{3,2},{4,7},{5,4},{6,5},{7,6},{8,11},{9,8},{10,9... | collective-permute-start | bytes 3096584 | tf_op jit(solution)/shard_map/ppermute | solution.py:273
  25.8 1.0 maximum_maximum_fusion.refs_0_
  26.8 0.1 collective-permute-start.4
  26.9 2.7 %collective-permute-start.5 = (f32[4,63,8,128]{3,2,1,0:T(8,128)S(1)}, f32[4,63,8,128]{3,2,1,0:T(8,128)S(1)}, u32[]{:S(2)}, u32[]{:S(2)}) collective-permute-start(f32[4,63,8,128]{3,2,1,0:T(8,128)S(1)} %maximum_maximum_fusion.refs_0_), channel_id=1, source_target_pairs={{0,24},{1,25},{2,26},{3,27},{4,28},{5,29},{6,30},{7,31},{8,0},{9,1... | collective-permute-start | bytes 3096584 | tf_op jit(solution)/shard_map/ppermute | solution.py:273
  29.5 1.9 collective-permute-done.9.refs_2_
  31.5 1.3 collective-permute-start.10
  32.8 13.2 %collective-permute-done.17.refs_1_ = f32[4,63,8,128]{3,2,1,0:T(8,128)S(1)} collective-permute-done((f32[4,63,8,128]{3,2,1,0:T(8,128)S(1)}, f32[4,63,8,128]{3,2,1,0:T(8,128)S(1)}, u32[]{:S(2)}, u32[]{:S(2)}) %collective-permute-start.17) | collective-permute-done | bytes 1032224 | tf_op jit(solution)/shard_map/ppermute | solution.py:273
  46.1 2.7 %collective-permute-start.20 = (f32[2,63,8,128]{3,2,1,0:T(8,128)S(1)}, f32[2,63,8,128]{3,2,1,0:T(8,128)S(1)}, u32[]{:S(2)}, u32[]{:S(2)}) collective-permute-start(f32[2,63,8,128]{3,2,1,0:T(8,128)S(1)} %slice.47), channel_id=1, source_target_pairs={{0,3},{1,0},{2,1},{3,2},{4,7},{5,4},{6,5},{7,6},{8,11},{9,8},{10,9... | collective-permute-start | bytes 1548296 | tf_op jit(solution)/shard_map/ppermute | solution.py:273
  48.9 0.3 collective-permute-done.4.refs_1_
  49.2 0.1 collective-permute-start.6
  49.4 2.7 %collective-permute-start.7 = (f32[2,63,8,128]{3,2,1,0:T(8,128)S(1)}, f32[2,63,8,128]{3,2,1,0:T(8,128)S(1)}, u32[]{:S(2)}, u32[]{:S(2)}) collective-permute-start(f32[2,63,8,128]{3,2,1,0:T(8,128)S(1)} %slice.43), channel_id=1, source_target_pairs={{0,24},{1,25},{2,26},{3,27},{4,28},{5,29},{6,30},{7,31},{8,0},{9,1... | collective-permute-start | bytes 1548296 | tf_op jit(solution)/shard_map/ppermute | solution.py:273
  52.2 0.7 collective-permute-done.10.refs_5_
  52.9 1.3 collective-permute-start.31
  54.2 2.8 %collective-permute-done.19.refs_3_ = f32[2,63,8,128]{3,2,1,0:T(8,128)S(1)} collective-permute-done((f32[2,63,8,128]{3,2,1,0:T(8,128)S(1)}, f32[2,63,8,128]{3,2,1,0:T(8,128)S(1)}, u32[]{:S(2)}, u32[]{:S(2)}) %collective-permute-start.19) | collective-permute-done | bytes 516128 | tf_op jit(solution)/shard_map/ppermute | solution.py:273
  57.0 2.7 %collective-permute-start.34 = (f32[2,63,8,128]{3,2,1,0:T(8,128)S(1)}, f32[2,63,8,128]{3,2,1,0:T(8,128)S(1)}, u32[]{:S(2)}, u32[]{:S(2)}) collective-permute-start(f32[2,63,8,128]{3,2,1,0:T(8,128)S(1)} %collective-permute-done.9.refs_2_), channel_id=1, source_target_pairs={{0,3},{1,0},{2,1},{3,2},{4,7},{5,4},{6,5},{7,6},{8,11},{9,8},{10,9... | collective-permute-start | bytes 1548296 | tf_op jit(solution)/shard_map/ppermute | solution.py:273
  59.8 2.7 %collective-permute-start.25 = (f32[4,63,8,128]{3,2,1,0:T(8,128)}, f32[4,63,8,128]{3,2,1,0:T(8,128)}, u32[]{:S(2)}, u32[]{:S(2)}) collective-permute-start(f32[4,63,8,128]{3,2,1,0:T(8,128)} %collective-permute-done.10.refs_5_), channel_id=1, source_target_pairs={{0,24},{1,25},{2,26},{3,27},{4,28},{5,29},{6,30},{7,31},{8,0},{9,1... | collective-permute-start | bytes 3096584 | tf_op jit(solution)/shard_map/ppermute | solution.py:273
  62.5 0.6 collective-permute-done.31.refs_3_
  63.1 4.1 %collective-permute-done.32.refs_4_ = f32[2,63,8,128]{3,2,1,0:T(8,128)S(1)} collective-permute-done((f32[2,63,8,128]{3,2,1,0:T(8,128)S(1)}, f32[2,63,8,128]{3,2,1,0:T(8,128)S(1)}, u32[]{:S(2)}, u32[]{:S(2)}) %collective-permute-start.32) | collective-permute-done | bytes 516128 | tf_op jit(solution)/shard_map/ppermute | solution.py:273
  67.2 0.7 copy-done.8
  68.0 0.8 copy-done.10
  68.7 1.9 collective-permute-start.35
  70.7 23.5 %copy.3.w_ref = f32[6400,800]{1,0:T(8,128)} copy(f32[6400,800]{0,1:T(8,128)} %param.3) | data formatting | bytes 40960000 | tf_op jit(solution)/shard_map/optimization_barrier | solution.py:277
  94.2 21.0 %split_w.1 = (bf16[6400,896]{1,0:T(8,128)(2,1)}, bf16[6400,768]{1,0:T(8,128)(2,1)}) custom-call(f32[6400,800]{1,0:T(8,128)} %copy.3.w_ref), custom_call_target="tpu_custom_call" | custom-call | flops 20000000 | bytes 44000000 | tf_op jit(solution)/shard_map/split_w/pallas_call | solution.py:88
  115.2 13.9 %product.5 = (f32[40,800]{1,0:T(8,128)}, f32[40,800]{1,0:T(8,128)}, f32[40,800]{1,0:T(8,128)}, f32[40,800]{1,0:T(8,128)}) custom-call(s32[5]{0:T(128)} %stack.23.sc_ref, f32[4,63,8,128]{3,2,1,0:T(8,128)} %copy-done.1, f32[4,63,8,128]{3,2,1,0:T(8,128)} %copy-done.5, f32[4,63,8,128]{3,2,1,0:T(8,128)} %copy-done.6, f32[2,63,8,128]{3,2,1,0:T(8,128)} %copy-done.17, ...), custom_call_target="tpu_custom_call" | custom-call | flops 4915200000 | bytes 22000000 | tf_op jit(solution)/shard_map/product/pallas_call | solution.py:207
  129.1 6.7 %collective-permute-start.21 = (f32[40,800]{1,0:T(8,128)}, f32[40,800]{1,0:T(8,128)S(1)}, u32[]{:S(2)}, u32[]{:S(2)}) collective-permute-start(f32[40,800]{1,0:T(8,128)} %get-tuple-element.46), channel_id=1, source_target_pairs={{0,32},{32,0},{64,96},{96,64},{1,33},{33,1},{65,97},{97,65},{2,34}... | collective-permute-start | bytes 384008 | tf_op jit(solution)/shard_map/ppermute | solution.py:281
  135.9 0.1 collective-permute-start.29
  136.0 1.3 slice.49
  137.3 2.5 %collective-permute-start.30 = (f32[2,63,8,128]{3,2,1,0:T(8,128)S(1)}, f32[2,63,8,128]{3,2,1,0:T(8,128)S(1)}, u32[]{:S(2)}, u32[]{:S(2)}) collective-permute-start(f32[2,63,8,128]{3,2,1,0:T(8,128)S(1)} %slice.49), channel_id=1, source_target_pairs={{0,24},{1,25},{2,26},{3,27},{4,28},{5,29},{6,30},{7,31},{8,0},{9,1... | collective-permute-start | bytes 1548296 | tf_op jit(solution)/shard_map/ppermute | solution.py:273
  139.8 2.6 %collective-permute-start.37 = (f32[2,63,8,128]{3,2,1,0:T(8,128)}, f32[2,63,8,128]{3,2,1,0:T(8,128)S(1)}, u32[]{:S(2)}, u32[]{:S(2)}) collective-permute-start(f32[2,63,8,128]{3,2,1,0:T(8,128)} %collective-permute-done.35.refs_7_), channel_id=1, source_target_pairs={{0,3},{1,0},{2,1},{3,2},{4,7},{5,4},{6,5},{7,6},{8,11},{9,8},{10,9... | collective-permute-start | bytes 1548296 | tf_op jit(solution)/shard_map/ppermute | solution.py:273
  142.5 15.2 %product.4 = (f32[50,800]{1,0:T(8,128)}, f32[50,800]{1,0:T(8,128)}, f32[50,800]{1,0:T(8,128)}, f32[50,800]{1,0:T(8,128)}) custom-call(s32[5]{0:T(128)} %stack.23.sc_ref, f32[4,63,8,128]{3,2,1,0:T(8,128)} %copy-done, f32[4,63,8,128]{3,2,1,0:T(8,128)} %copy-done.3, f32[4,63,8,128]{3,2,1,0:T(8,128)} %copy-done.4, f32[2,63,8,128]{3,2,1,0:T(8,128)} %copy-done.11, ...), custom_call_target="tpu_custom_call" | custom-call | flops 6144000000 | bytes 22000000 | tf_op jit(solution)/shard_map/product/pallas_call | solution.py:207
  157.7 2.7 %collective-permute-start.22 = (f32[40,800]{1,0:T(8,128)S(1)}, f32[40,800]{1,0:T(8,128)S(1)}, u32[]{:S(2)}, u32[]{:S(2)}) collective-permute-start(f32[40,800]{1,0:T(8,128)S(1)} %copy-done.33), channel_id=1, source_target_pairs={{0,64},{32,96},{64,0},{96,32},{1,65},{33,97},{65,1},{97,33},{2,66}... | collective-permute-start | bytes 384008 | tf_op jit(solution)/shard_map/ppermute | solution.py:281
  160.4 1.8 collective-permute-start.23
  162.3 2.9 %collective-permute-start.15 = (f32[50,800]{1,0:T(8,128)}, f32[50,800]{1,0:T(8,128)S(1)}, u32[]{:S(2)}, u32[]{:S(2)}) collective-permute-start(f32[50,800]{1,0:T(8,128)} %get-tuple-element.43), channel_id=1, source_target_pairs={{0,64},{32,96},{64,0},{96,32},{1,65},{33,97},{65,1},{97,33},{2,66}... | collective-permute-start | bytes 480008 | tf_op jit(solution)/shard_map/ppermute | solution.py:281
  165.2 15.2 %product.7 = (f32[50,800]{1,0:T(8,128)}, f32[50,800]{1,0:T(8,128)}, f32[50,800]{1,0:T(8,128)}, f32[50,800]{1,0:T(8,128)}) custom-call(s32[5]{0:T(128)} %stack.23.sc_ref, f32[2,63,8,128]{3,2,1,0:T(8,128)} %copy-done.14, f32[2,63,8,128]{3,2,1,0:T(8,128)} %copy-done.15, f32[2,63,8,128]{3,2,1,0:T(8,128)} %copy-done.7, ...), custom_call_target="tpu_custom_call" | custom-call | flops 6144000000 | bytes 22000000 | tf_op jit(solution)/shard_map/product/pallas_call | solution.py:207
  180.5 0.9 collective-permute-start.16
  181.4 0.2 collective-permute-start.38
  181.6 2.4 %collective-permute-start.39 = (f32[50,800]{1,0:T(8,128)}, f32[50,800]{1,0:T(8,128)S(1)}, u32[]{:S(2)}, u32[]{:S(2)}) collective-permute-start(f32[50,800]{1,0:T(8,128)} %get-tuple-element.63), channel_id=1, source_target_pairs={{0,64},{32,96},{64,0},{96,32},{1,65},{33,97},{65,1},{97,33},{2,66}... | collective-permute-start | bytes 480008 | tf_op jit(solution)/shard_map/ppermute | solution.py:281
  184.0 1.1 collective-permute-start.40
  185.1 12.0 %product.6 = (f32[20,800]{1,0:T(8,128)}, f32[20,800]{1,0:T(8,128)}, f32[20,800]{1,0:T(8,128)}, f32[20,800]{1,0:T(8,128)}) custom-call(s32[5]{0:T(128)} %stack.23.sc_ref, f32[4,63,8,128]{3,2,1,0:T(8,128)} %copy-done.2, f32[4,63,8,128]{3,2,1,0:T(8,128)} %collective-permute-done.25.refs_1_, ...), custom_call_target="tpu_custom_call" | custom-call | flops 2457600000 | bytes 22000000 | tf_op jit(solution)/shard_map/product/pallas_call | solution.py:207
  197.1 0.1 collective-permute-start.26
  197.2 2.6 %collective-permute-start.27 = (f32[20,800]{1,0:T(8,128)}, f32[20,800]{1,0:T(8,128)S(1)}, u32[]{:S(2)}, u32[]{:S(2)}) collective-permute-start(f32[20,800]{1,0:T(8,128)} %get-tuple-element.53), channel_id=1, source_target_pairs={{0,64},{32,96},{64,0},{96,32},{1,65},{33,97},{65,1},{97,33},{2,66}... | collective-permute-start | bytes 192008 | tf_op jit(solution)/shard_map/ppermute | solution.py:281
  199.7 1.4 collective-permute-start.28
  201.2 1.5 collective-permute-done.27.refs_10_
  202.7 3.9 %collective-permute-done.28.refs_11_ = f32[20,800]{1,0:T(8,128)S(1)} collective-permute-done((f32[20,800]{1,0:T(8,128)}, f32[20,800]{1,0:T(8,128)S(1)}, u32[]{:S(2)}, u32[]{:S(2)}) %collective-permute-start.28) | collective-permute-done | bytes 64032 | tf_op jit(solution)/shard_map/ppermute | solution.py:281
  206.7 0.5 copy-done.30
  207.2 0.1 copy-done.22
  207.3 0.1 copy-done.23
  207.4 0.1 copy-done.24
  207.4 2.9 %place.1 = f32[160,800]{1,0:T(8,128)} custom-call(s32[5]{0:T(128)} %stack.23.sc_ref, f32[50,800]{1,0:T(8,128)} %get-tuple-element.41.refs_0_, f32[50,800]{1,0:T(8,128)} %copy-done.19, f32[50,800]{1,0:T(8,128)} %copy-done.20, f32[50,800]{1,0:T(8,128)} %copy-done.21, f32[40,800]{1,0:T(8,128)} %get-tuple-element.45.refs_4_, f32[40,800]{1,0:T(8,128)} %copy-done.25, ...), custom_call_target="tpu_custom_call" | custom-call | flops 1000000 | bytes 3000000 | tf_op jit(solution)/shard_map/place/pallas_call | solution.py:249
  (111 shorter events, 0.7 us)
Async XLA Ops:
  3.1 10.7 %collective-permute-start.8 = (f32[1,63,8,128]{3,2,1,0:T(8,128)}, f32[1,63,8,128]{3,2,1,0:T(8,128)S(1)}, u32[]{:S(2)}, u32[]{:S(2)}) collective-permute-start(f32[1,63,8,128]{3,2,1,0:T(8,128)} %bitcast.7), channel_id=1, source_target_pairs={{0,8},{1,9},{2,10},{3,11},{4,12},{5,13},{6,14},{7,15},{8,16},{9,17... | collective-permute-start | bytes 774152 | tf_op jit(solution)/shard_map/ppermute | solution.py:273
  5.6 8.4 %collective-permute-start.11 = (f32[1,63,8,128]{3,2,1,0:T(8,128)}, f32[1,63,8,128]{3,2,1,0:T(8,128)S(1)}, u32[]{:S(2)}, u32[]{:S(2)}) collective-permute-start(f32[1,63,8,128]{3,2,1,0:T(8,128)} %bitcast.8), channel_id=1, source_target_pairs={{0,24},{1,25},{2,26},{3,27},{4,28},{5,29},{6,30},{7,31},{8,0},{9,1... | collective-permute-start | bytes 774152 | tf_op jit(solution)/shard_map/ppermute | solution.py:273
  7.7 9.0 %collective-permute-start = (f32[1,63,8,128]{3,2,1,0:T(8,128)}, f32[1,63,8,128]{3,2,1,0:T(8,128)S(1)}, u32[]{:S(2)}, u32[]{:S(2)}) collective-permute-start(f32[1,63,8,128]{3,2,1,0:T(8,128)} %bitcast.11), channel_id=1, source_target_pairs={{0,1},{1,2},{2,3},{3,0},{4,5},{5,6},{6,7},{7,4},{8,9},{9,10},{10,1... | collective-permute-start | bytes 774152 | tf_op jit(solution)/shard_map/ppermute | solution.py:273
  8.9 9.1 %collective-permute-start.1 = (f32[1,63,8,128]{3,2,1,0:T(8,128)}, f32[1,63,8,128]{3,2,1,0:T(8,128)S(1)}, u32[]{:S(2)}, u32[]{:S(2)}) collective-permute-start(f32[1,63,8,128]{3,2,1,0:T(8,128)} %bitcast.12), channel_id=1, source_target_pairs={{0,3},{1,0},{2,1},{3,2},{4,7},{5,4},{6,5},{7,6},{8,11},{9,8},{10,9... | collective-permute-start | bytes 774152 | tf_op jit(solution)/shard_map/ppermute | solution.py:273
  13.9 8.0 %collective-permute-start.12 = (f32[1,32,8,128]{3,2,1,0:T(8,128)S(1)}, f32[1,32,8,128]{3,2,1,0:T(8,128)S(1)}, u32[]{:S(2)}, u32[]{:S(2)}) collective-permute-start(f32[1,32,8,128]{3,2,1,0:T(8,128)S(1)} %slice.44), channel_id=1, source_target_pairs={{0,8},{1,9},{2,10},{3,11},{4,12},{5,13},{6,14},{7,15},{8,16},{9,17... | collective-permute-start | bytes 393224 | tf_op jit(solution)/shard_map/ppermute | solution.py:273
  14.0 8.0 %collective-permute-start.13 = (f32[1,31,8,128]{3,2,1,0:T(8,128)S(1)}, f32[1,31,8,128]{3,2,1,0:T(8,128)S(1)}, u32[]{:S(2)}, u32[]{:S(2)}) collective-permute-start(f32[1,31,8,128]{3,2,1,0:T(8,128)S(1)} %slice.45), channel_id=1, source_target_pairs={{0,24},{1,25},{2,26},{3,27},{4,28},{5,29},{6,30},{7,31},{8,0},{9,1... | collective-permute-start | bytes 380936 | tf_op jit(solution)/shard_map/ppermute | solution.py:273
  16.7 9.1 %collective-permute-start.2 = (f32[1,32,8,128]{3,2,1,0:T(8,128)S(1)}, f32[1,32,8,128]{3,2,1,0:T(8,128)S(1)}, u32[]{:S(2)}, u32[]{:S(2)}) collective-permute-start(f32[1,32,8,128]{3,2,1,0:T(8,128)S(1)} %slice.40), channel_id=1, source_target_pairs={{0,1},{1,2},{2,3},{3,0},{4,5},{5,6},{6,7},{7,4},{8,9},{9,10},{10,1... | collective-permute-start | bytes 393224 | tf_op jit(solution)/shard_map/ppermute | solution.py:273
  18.0 7.8 %collective-permute-start.3 = (f32[1,31,8,128]{3,2,1,0:T(8,128)S(1)}, f32[1,31,8,128]{3,2,1,0:T(8,128)S(1)}, u32[]{:S(2)}, u32[]{:S(2)}) collective-permute-start(f32[1,31,8,128]{3,2,1,0:T(8,128)S(1)} %slice.41), channel_id=1, source_target_pairs={{0,3},{1,0},{2,1},{3,2},{4,7},{5,4},{6,5},{7,6},{8,11},{9,8},{10,9... | collective-permute-start | bytes 380936 | tf_op jit(solution)/shard_map/ppermute | solution.py:273
  20.5 11.0 %collective-permute-start.9 = (f32[2,63,8,128]{3,2,1,0:T(8,128)S(1)}, f32[2,63,8,128]{3,2,1,0:T(8,128)S(1)}, u32[]{:S(2)}, u32[]{:S(2)}) collective-permute-start(f32[2,63,8,128]{3,2,1,0:T(8,128)S(1)} %pad_maximum_fusion.1), channel_id=1, source_target_pairs={{0,4},{1,5},{2,6},{3,7},{4,0},{5,1},{6,2},{7,3},{8,12},{9,13},{10,... | collective-permute-start | bytes 1548296 | tf_op jit(solution)/shard_map/ppermute | solution.py:273
  23.0 71.2 %copy-start.1 = (f32[4,63,8,128]{3,2,1,0:T(8,128)}, f32[4,63,8,128]{3,2,1,0:T(8,128)S(1)}, u32[]{:S(2)}) copy-start(f32[4,63,8,128]{3,2,1,0:T(8,128)S(1)} %pad_maximum_fusion.refs_0_) | copy-start | bytes 3096580
  23.0 23.0 %collective-permute-start.17 = (f32[4,63,8,128]{3,2,1,0:T(8,128)S(1)}, f32[4,63,8,128]{3,2,1,0:T(8,128)S(1)}, u32[]{:S(2)}, u32[]{:S(2)}) collective-permute-start(f32[4,63,8,128]{3,2,1,0:T(8,128)S(1)} %pad_maximum_fusion.refs_0_), channel_id=1, source_target_pairs={{0,1},{1,2},{2,3},{3,0},{4,5},{5,6},{6,7},{7,4},{8,9},{9,10},{10,1... | collective-permute-start | bytes 3096584 | tf_op jit(solution)/shard_map/ppermute | solution.py:273
  23.1 23.0 %collective-permute-start.18 = (f32[4,63,8,128]{3,2,1,0:T(8,128)S(1)}, f32[4,63,8,128]{3,2,1,0:T(8,128)S(1)}, u32[]{:S(2)}, u32[]{:S(2)}) collective-permute-start(f32[4,63,8,128]{3,2,1,0:T(8,128)S(1)} %pad_maximum_fusion.refs_0_), channel_id=1, source_target_pairs={{0,3},{1,0},{2,1},{3,2},{4,7},{5,4},{6,5},{7,6},{8,11},{9,8},{10,9... | collective-permute-start | bytes 3096584 | tf_op jit(solution)/shard_map/ppermute | solution.py:273
  26.8 67.4 %copy-start = (f32[4,63,8,128]{3,2,1,0:T(8,128)}, f32[4,63,8,128]{3,2,1,0:T(8,128)S(1)}, u32[]{:S(2)}) copy-start(f32[4,63,8,128]{3,2,1,0:T(8,128)S(1)} %maximum_maximum_fusion.refs_0_) | copy-start | bytes 3096580
  26.8 22.4 %collective-permute-start.4 = (f32[4,63,8,128]{3,2,1,0:T(8,128)S(1)}, f32[4,63,8,128]{3,2,1,0:T(8,128)S(1)}, u32[]{:S(2)}, u32[]{:S(2)}) collective-permute-start(f32[4,63,8,128]{3,2,1,0:T(8,128)S(1)} %maximum_maximum_fusion.refs_0_), channel_id=1, source_target_pairs={{0,8},{1,9},{2,10},{3,11},{4,12},{5,13},{6,14},{7,15},{8,16},{9,17... | collective-permute-start | bytes 3096584 | tf_op jit(solution)/shard_map/ppermute | solution.py:273
  26.9 22.4 %collective-permute-start.5 = (f32[4,63,8,128]{3,2,1,0:T(8,128)S(1)}, f32[4,63,8,128]{3,2,1,0:T(8,128)S(1)}, u32[]{:S(2)}, u32[]{:S(2)}) collective-permute-start(f32[4,63,8,128]{3,2,1,0:T(8,128)S(1)} %maximum_maximum_fusion.refs_0_), channel_id=1, source_target_pairs={{0,24},{1,25},{2,26},{3,27},{4,28},{5,29},{6,30},{7,31},{8,0},{9,1... | collective-permute-start | bytes 3096584 | tf_op jit(solution)/shard_map/ppermute | solution.py:273
  31.5 31.0 %copy-start.7 = (f32[2,63,8,128]{3,2,1,0:T(8,128)}, f32[2,63,8,128]{3,2,1,0:T(8,128)S(1)}, u32[]{:S(2)}) copy-start(f32[2,63,8,128]{3,2,1,0:T(8,128)S(1)} %collective-permute-done.9.refs_2_) | copy-start | bytes 1548292
  31.5 21.4 %collective-permute-start.10 = (f32[4,63,8,128]{3,2,1,0:T(8,128)S(1)}, f32[4,63,8,128]{3,2,1,0:T(8,128)}, u32[]{:S(2)}, u32[]{:S(2)}) collective-permute-start(f32[4,63,8,128]{3,2,1,0:T(8,128)S(1)} %maximum_maximum_fusion.refs_0_), channel_id=1, source_target_pairs={{0,4},{1,5},{2,6},{3,7},{4,0},{5,1},{6,2},{7,3},{8,12},{9,13},{10,... | collective-permute-start | bytes 3096584 | tf_op jit(solution)/shard_map/ppermute | solution.py:273
  46.0 13.8 %copy-start.5 = (f32[4,63,8,128]{3,2,1,0:T(8,128)}, f32[4,63,8,128]{3,2,1,0:T(8,128)S(1)}, u32[]{:S(2)}) copy-start(f32[4,63,8,128]{3,2,1,0:T(8,128)S(1)} %collective-permute-done.17.refs_1_) | copy-start | bytes 3096580
  46.0 11.0 %collective-permute-start.19 = (f32[2,63,8,128]{3,2,1,0:T(8,128)S(1)}, f32[2,63,8,128]{3,2,1,0:T(8,128)S(1)}, u32[]{:S(2)}, u32[]{:S(2)}) collective-permute-start(f32[2,63,8,128]{3,2,1,0:T(8,128)S(1)} %slice.46), channel_id=1, source_target_pairs={{0,1},{1,2},{2,3},{3,0},{4,5},{5,6},{6,7},{7,4},{8,9},{9,10},{10,1... | collective-permute-start | bytes 1548296 | tf_op jit(solution)/shard_map/ppermute | solution.py:273
  46.1 13.7 %copy-start.6 = (f32[4,63,8,128]{3,2,1,0:T(8,128)}, f32[4,63,8,128]{3,2,1,0:T(8,128)S(1)}, u32[]{:S(2)}) copy-start(f32[4,63,8,128]{3,2,1,0:T(8,128)S(1)} %collective-permute-done.18.refs_2_) | copy-start | bytes 3096580
  46.1 10.8 %collective-permute-start.20 = (f32[2,63,8,128]{3,2,1,0:T(8,128)S(1)}, f32[2,63,8,128]{3,2,1,0:T(8,128)S(1)}, u32[]{:S(2)}, u32[]{:S(2)}) collective-permute-start(f32[2,63,8,128]{3,2,1,0:T(8,128)S(1)} %slice.47), channel_id=1, source_target_pairs={{0,3},{1,0},{2,1},{3,2},{4,7},{5,4},{6,5},{7,6},{8,11},{9,8},{10,9... | collective-permute-start | bytes 1548296 | tf_op jit(solution)/shard_map/ppermute | solution.py:273
  49.2 10.5 %copy-start.3 = (f32[4,63,8,128]{3,2,1,0:T(8,128)}, f32[4,63,8,128]{3,2,1,0:T(8,128)S(1)}, u32[]{:S(2)}) copy-start(f32[4,63,8,128]{3,2,1,0:T(8,128)S(1)} %collective-permute-done.4.refs_1_) | copy-start | bytes 3096580
  49.2 10.4 %collective-permute-start.6 = (f32[2,63,8,128]{3,2,1,0:T(8,128)S(1)}, f32[2,63,8,128]{3,2,1,0:T(8,128)S(1)}, u32[]{:S(2)}, u32[]{:S(2)}) collective-permute-start(f32[2,63,8,128]{3,2,1,0:T(8,128)S(1)} %slice.42), channel_id=1, source_target_pairs={{0,8},{1,9},{2,10},{3,11},{4,12},{5,13},{6,14},{7,15},{8,16},{9,17... | collective-permute-start | bytes 1548296 | tf_op jit(solution)/shard_map/ppermute | solution.py:273
  49.3 10.3 %copy-start.4 = (f32[4,63,8,128]{3,2,1,0:T(8,128)}, f32[4,63,8,128]{3,2,1,0:T(8,128)S(1)}, u32[]{:S(2)}) copy-start(f32[4,63,8,128]{3,2,1,0:T(8,128)S(1)} %collective-permute-done.5.refs_2_) | copy-start | bytes 3096580
  49.4 10.4 %collective-permute-start.7 = (f32[2,63,8,128]{3,2,1,0:T(8,128)S(1)}, f32[2,63,8,128]{3,2,1,0:T(8,128)S(1)}, u32[]{:S(2)}, u32[]{:S(2)}) collective-permute-start(f32[2,63,8,128]{3,2,1,0:T(8,128)S(1)} %slice.43), channel_id=1, source_target_pairs={{0,24},{1,25},{2,26},{3,27},{4,28},{5,29},{6,30},{7,31},{8,0},{9,1... | collective-permute-start | bytes 1548296 | tf_op jit(solution)/shard_map/ppermute | solution.py:273
  52.9 10.2 %collective-permute-start.31 = (f32[2,63,8,128]{3,2,1,0:T(8,128)S(1)}, f32[2,63,8,128]{3,2,1,0:T(8,128)}, u32[]{:S(2)}, u32[]{:S(2)}) collective-permute-start(f32[2,63,8,128]{3,2,1,0:T(8,128)S(1)} %pad_maximum_fusion.2), channel_id=1, source_target_pairs={{0,4},{1,5},{2,6},{3,7},{4,0},{5,1},{6,2},{7,3},{8,12},{9,13},{10,... | collective-permute-start | bytes 1548296 | tf_op jit(solution)/shard_map/ppermute | solution.py:273
  57.0 10.2 %copy-start.17 = (f32[2,63,8,128]{3,2,1,0:T(8,128)}, f32[2,63,8,128]{3,2,1,0:T(8,128)S(1)}, u32[]{:S(2)}) copy-start(f32[2,63,8,128]{3,2,1,0:T(8,128)S(1)} %collective-permute-done.19.refs_3_) | copy-start | bytes 1548292
  57.0 10.2 %collective-permute-start.32 = (f32[2,63,8,128]{3,2,1,0:T(8,128)S(1)}, f32[2,63,8,128]{3,2,1,0:T(8,128)S(1)}, u32[]{:S(2)}, u32[]{:S(2)}) collective-permute-start(f32[2,63,8,128]{3,2,1,0:T(8,128)S(1)} %collective-permute-done.9.refs_2_), channel_id=1, source_target_pairs={{0,1},{1,2},{2,3},{3,0},{4,5},{5,6},{6,7},{7,4},{8,9},{9,10},{10,1... | collective-permute-start | bytes 1548296 | tf_op jit(solution)/shard_map/ppermute | solution.py:273
  57.0 10.2 %copy-start.18 = (f32[2,63,8,128]{3,2,1,0:T(8,128)}, f32[2,63,8,128]{3,2,1,0:T(8,128)S(1)}, u32[]{:S(2)}) copy-start(f32[2,63,8,128]{3,2,1,0:T(8,128)S(1)} %collective-permute-done.20.refs_4_) | copy-start | bytes 1548292
  57.0 10.2 %collective-permute-start.34 = (f32[2,63,8,128]{3,2,1,0:T(8,128)S(1)}, f32[2,63,8,128]{3,2,1,0:T(8,128)S(1)}, u32[]{:S(2)}, u32[]{:S(2)}) collective-permute-start(f32[2,63,8,128]{3,2,1,0:T(8,128)S(1)} %collective-permute-done.9.refs_2_), channel_id=1, source_target_pairs={{0,3},{1,0},{2,1},{3,2},{4,7},{5,4},{6,5},{7,6},{8,11},{9,8},{10,9... | collective-permute-start | bytes 1548296 | tf_op jit(solution)/shard_map/ppermute | solution.py:273
  59.7 7.5 %copy-start.11 = (f32[2,63,8,128]{3,2,1,0:T(8,128)}, f32[2,63,8,128]{3,2,1,0:T(8,128)S(1)}, u32[]{:S(2)}) copy-start(f32[2,63,8,128]{3,2,1,0:T(8,128)S(1)} %collective-permute-done.6.refs_3_) | copy-start | bytes 1548292
  59.7 76.2 %collective-permute-start.24 = (f32[4,63,8,128]{3,2,1,0:T(8,128)}, f32[4,63,8,128]{3,2,1,0:T(8,128)S(1)}, u32[]{:S(2)}, u32[]{:S(2)}) collective-permute-start(f32[4,63,8,128]{3,2,1,0:T(8,128)} %collective-permute-done.10.refs_5_), channel_id=1, source_target_pairs={{0,8},{1,9},{2,10},{3,11},{4,12},{5,13},{6,14},{7,15},{8,16},{9,17... | collective-permute-start | bytes 3096584 | tf_op jit(solution)/shard_map/ppermute | solution.py:273
  59.8 7.4 %copy-start.12 = (f32[2,63,8,128]{3,2,1,0:T(8,128)}, f32[2,63,8,128]{3,2,1,0:T(8,128)S(1)}, u32[]{:S(2)}) copy-start(f32[2,63,8,128]{3,2,1,0:T(8,128)S(1)} %collective-permute-done.7.refs_4_) | copy-start | bytes 1548292
  59.8 76.2 %collective-permute-start.25 = (f32[4,63,8,128]{3,2,1,0:T(8,128)}, f32[4,63,8,128]{3,2,1,0:T(8,128)}, u32[]{:S(2)}, u32[]{:S(2)}) collective-permute-start(f32[4,63,8,128]{3,2,1,0:T(8,128)} %collective-permute-done.10.refs_5_), channel_id=1, source_target_pairs={{0,24},{1,25},{2,26},{3,27},{4,28},{5,29},{6,30},{7,31},{8,0},{9,1... | collective-permute-start | bytes 3096584 | tf_op jit(solution)/shard_map/ppermute | solution.py:273
  67.2 68.7 %collective-permute-start.33 = (f32[2,63,8,128]{3,2,1,0:T(8,128)}, f32[2,63,8,128]{3,2,1,0:T(8,128)}, u32[]{:S(2)}, u32[]{:S(2)}) collective-permute-start(f32[2,63,8,128]{3,2,1,0:T(8,128)} %collective-permute-done.31.refs_3_), channel_id=1, source_target_pairs={{0,1},{1,2},{2,3},{3,0},{4,5},{5,6},{6,7},{7,4},{8,9},{9,10},{10,1... | collective-permute-start | bytes 1548296 | tf_op jit(solution)/shard_map/ppermute | solution.py:273
  68.7 71.1 %collective-permute-start.35 = (f32[2,63,8,128]{3,2,1,0:T(8,128)}, f32[2,63,8,128]{3,2,1,0:T(8,128)}, u32[]{:S(2)}, u32[]{:S(2)}) collective-permute-start(f32[2,63,8,128]{3,2,1,0:T(8,128)} %collective-permute-done.31.refs_3_), channel_id=1, source_target_pairs={{0,3},{1,0},{2,1},{3,2},{4,7},{5,4},{6,5},{7,6},{8,11},{9,8},{10,9... | collective-permute-start | bytes 1548296 | tf_op jit(solution)/shard_map/ppermute | solution.py:273
  94.2 41.7 %copy-start.9 = (f32[2,63,8,128]{3,2,1,0:T(8,128)S(1)}, f32[2,63,8,128]{3,2,1,0:T(8,128)}, u32[]{:S(2)}) copy-start(f32[2,63,8,128]{3,2,1,0:T(8,128)} %copy-done.8) | copy-start | bytes 1548292
  129.1 28.6 %copy-start.33 = (f32[40,800]{1,0:T(8,128)S(1)}, f32[40,800]{1,0:T(8,128)}, u32[]{:S(2)}) copy-start(f32[40,800]{1,0:T(8,128)} %get-tuple-element.47) | copy-start | bytes 384004
  129.1 31.3 %copy-start.32 = (f32[40,800]{1,0:T(8,128)S(1)}, f32[40,800]{1,0:T(8,128)}, u32[]{:S(2)}) copy-start(f32[40,800]{1,0:T(8,128)} %get-tuple-element.48) | copy-start | bytes 384004
  129.1 51.3 %collective-permute-start.21 = (f32[40,800]{1,0:T(8,128)}, f32[40,800]{1,0:T(8,128)S(1)}, u32[]{:S(2)}, u32[]{:S(2)}) collective-permute-start(f32[40,800]{1,0:T(8,128)} %get-tuple-element.46), channel_id=1, source_target_pairs={{0,32},{32,0},{64,96},{96,64},{1,33},{33,1},{65,97},{97,65},{2,34}... | collective-permute-start | bytes 384008 | tf_op jit(solution)/shard_map/ppermute | solution.py:281
  135.8 21.9 %collective-permute-start.36 = (f32[2,63,8,128]{3,2,1,0:T(8,128)S(1)}, f32[2,63,8,128]{3,2,1,0:T(8,128)S(1)}, u32[]{:S(2)}, u32[]{:S(2)}) collective-permute-start(f32[2,63,8,128]{3,2,1,0:T(8,128)S(1)} %copy-done.9), channel_id=1, source_target_pairs={{0,1},{1,2},{2,3},{3,0},{4,5},{5,6},{6,7},{7,4},{8,9},{9,10},{10,1... | collective-permute-start | bytes 1548296 | tf_op jit(solution)/shard_map/ppermute | solution.py:273
  135.9 44.6 %copy-start.2 = (f32[4,63,8,128]{3,2,1,0:T(8,128)}, f32[4,63,8,128]{3,2,1,0:T(8,128)S(1)}, u32[]{:S(2)}) copy-start(f32[4,63,8,128]{3,2,1,0:T(8,128)S(1)} %collective-permute-done.24.refs_0_) | copy-start | bytes 3096580
  135.9 26.3 %collective-permute-start.29 = (f32[2,63,8,128]{3,2,1,0:T(8,128)S(1)}, f32[2,63,8,128]{3,2,1,0:T(8,128)S(1)}, u32[]{:S(2)}, u32[]{:S(2)}) collective-permute-start(f32[2,63,8,128]{3,2,1,0:T(8,128)S(1)} %slice.48), channel_id=1, source_target_pairs={{0,8},{1,9},{2,10},{3,11},{4,12},{5,13},{6,14},{7,15},{8,16},{9,17... | collective-permute-start | bytes 1548296 | tf_op jit(solution)/shard_map/ppermute | solution.py:273
  137.3 24.9 %collective-permute-start.30 = (f32[2,63,8,128]{3,2,1,0:T(8,128)S(1)}, f32[2,63,8,128]{3,2,1,0:T(8,128)S(1)}, u32[]{:S(2)}, u32[]{:S(2)}) collective-permute-start(f32[2,63,8,128]{3,2,1,0:T(8,128)S(1)} %slice.49), channel_id=1, source_target_pairs={{0,24},{1,25},{2,26},{3,27},{4,28},{5,29},{6,30},{7,31},{8,0},{9,1... | collective-permute-start | bytes 1548296 | tf_op jit(solution)/shard_map/ppermute | solution.py:273
  139.8 20.6 %collective-permute-start.37 = (f32[2,63,8,128]{3,2,1,0:T(8,128)}, f32[2,63,8,128]{3,2,1,0:T(8,128)S(1)}, u32[]{:S(2)}, u32[]{:S(2)}) collective-permute-start(f32[2,63,8,128]{3,2,1,0:T(8,128)} %collective-permute-done.35.refs_7_), channel_id=1, source_target_pairs={{0,3},{1,0},{2,1},{3,2},{4,7},{5,4},{6,5},{7,6},{8,11},{9,8},{10,9... | collective-permute-start | bytes 1548296 | tf_op jit(solution)/shard_map/ppermute | solution.py:273
  157.7 22.8 %copy-start.31 = (f32[50,800]{1,0:T(8,128)S(1)}, f32[50,800]{1,0:T(8,128)}, u32[]{:S(2)}) copy-start(f32[50,800]{1,0:T(8,128)} %get-tuple-element.44) | copy-start | bytes 480004
  157.7 7.5 %copy-start.13 = (f32[2,63,8,128]{3,2,1,0:T(8,128)}, f32[2,63,8,128]{3,2,1,0:T(8,128)S(1)}, u32[]{:S(2)}) copy-start(f32[2,63,8,128]{3,2,1,0:T(8,128)S(1)} %collective-permute-done.36.refs_8_) | copy-start | bytes 1548292
  157.7 23.7 %collective-permute-start.22 = (f32[40,800]{1,0:T(8,128)S(1)}, f32[40,800]{1,0:T(8,128)S(1)}, u32[]{:S(2)}, u32[]{:S(2)}) collective-permute-start(f32[40,800]{1,0:T(8,128)S(1)} %copy-done.33), channel_id=1, source_target_pairs={{0,64},{32,96},{64,0},{96,32},{1,65},{33,97},{65,1},{97,33},{2,66}... | collective-permute-start | bytes 384008 | tf_op jit(solution)/shard_map/ppermute | solution.py:281
  160.4 21.2 %collective-permute-start.23 = (f32[40,800]{1,0:T(8,128)S(1)}, f32[40,800]{1,0:T(8,128)S(1)}, u32[]{:S(2)}, u32[]{:S(2)}) collective-permute-start(f32[40,800]{1,0:T(8,128)S(1)} %copy-done.32), channel_id=1, source_target_pairs={{0,96},{32,64},{64,32},{96,0},{1,97},{33,65},{65,33},{97,1},{2,98}... | collective-permute-start | bytes 384008 | tf_op jit(solution)/shard_map/ppermute | solution.py:281
  162.2 21.8 %collective-permute-start.14 = (f32[50,800]{1,0:T(8,128)}, f32[50,800]{1,0:T(8,128)S(1)}, u32[]{:S(2)}, u32[]{:S(2)}) collective-permute-start(f32[50,800]{1,0:T(8,128)} %get-tuple-element.42), channel_id=1, source_target_pairs={{0,32},{32,0},{64,96},{96,64},{1,33},{33,1},{65,97},{97,65},{2,34}... | collective-permute-start | bytes 480008 | tf_op jit(solution)/shard_map/ppermute | solution.py:281
  162.3 34.8 %collective-permute-start.15 = (f32[50,800]{1,0:T(8,128)}, f32[50,800]{1,0:T(8,128)S(1)}, u32[]{:S(2)}, u32[]{:S(2)}) collective-permute-start(f32[50,800]{1,0:T(8,128)} %get-tuple-element.43), channel_id=1, source_target_pairs={{0,64},{32,96},{64,0},{96,32},{1,65},{33,97},{65,1},{97,33},{2,66}... | collective-permute-start | bytes 480008 | tf_op jit(solution)/shard_map/ppermute | solution.py:281
  180.5 26.1 %copy-start.25 = (f32[40,800]{1,0:T(8,128)}, f32[40,800]{1,0:T(8,128)S(1)}, u32[]{:S(2)}) copy-start(f32[40,800]{1,0:T(8,128)S(1)} %collective-permute-done.21.refs_5_) | copy-start | bytes 384004
  180.5 16.7 %collective-permute-start.16 = (f32[50,800]{1,0:T(8,128)S(1)}, f32[50,800]{1,0:T(8,128)S(1)}, u32[]{:S(2)}, u32[]{:S(2)}) collective-permute-start(f32[50,800]{1,0:T(8,128)S(1)} %copy-done.31), channel_id=1, source_target_pairs={{0,96},{32,64},{64,32},{96,0},{1,97},{33,65},{65,33},{97,1},{2,98}... | collective-permute-start | bytes 480008 | tf_op jit(solution)/shard_map/ppermute | solution.py:281
  181.4 25.2 %copy-start.26 = (f32[40,800]{1,0:T(8,128)}, f32[40,800]{1,0:T(8,128)S(1)}, u32[]{:S(2)}) copy-start(f32[40,800]{1,0:T(8,128)S(1)} %collective-permute-done.22.refs_6_) | copy-start | bytes 384004
  181.4 25.1 %collective-permute-start.38 = (f32[50,800]{1,0:T(8,128)}, f32[50,800]{1,0:T(8,128)S(1)}, u32[]{:S(2)}, u32[]{:S(2)}) collective-permute-start(f32[50,800]{1,0:T(8,128)} %get-tuple-element.62), channel_id=1, source_target_pairs={{0,32},{32,0},{64,96},{96,64},{1,33},{33,1},{65,97},{97,65},{2,34}... | collective-permute-start | bytes 480008 | tf_op jit(solution)/shard_map/ppermute | solution.py:281
  181.6 25.0 %copy-start.27 = (f32[40,800]{1,0:T(8,128)}, f32[40,800]{1,0:T(8,128)S(1)}, u32[]{:S(2)}) copy-start(f32[40,800]{1,0:T(8,128)S(1)} %collective-permute-done.23.refs_7_) | copy-start | bytes 384004
  181.6 25.0 %collective-permute-start.39 = (f32[50,800]{1,0:T(8,128)}, f32[50,800]{1,0:T(8,128)S(1)}, u32[]{:S(2)}, u32[]{:S(2)}) collective-permute-start(f32[50,800]{1,0:T(8,128)} %get-tuple-element.63), channel_id=1, source_target_pairs={{0,64},{32,96},{64,0},{96,32},{1,65},{33,97},{65,1},{97,33},{2,66}... | collective-permute-start | bytes 480008 | tf_op jit(solution)/shard_map/ppermute | solution.py:281
  184.0 22.6 %copy-start.19 = (f32[50,800]{1,0:T(8,128)}, f32[50,800]{1,0:T(8,128)S(1)}, u32[]{:S(2)}) copy-start(f32[50,800]{1,0:T(8,128)S(1)} %collective-permute-done.14.refs_1_) | copy-start | bytes 480004
  184.0 22.6 %collective-permute-start.40 = (f32[50,800]{1,0:T(8,128)}, f32[50,800]{1,0:T(8,128)S(1)}, u32[]{:S(2)}, u32[]{:S(2)}) collective-permute-start(f32[50,800]{1,0:T(8,128)} %get-tuple-element.64), channel_id=1, source_target_pairs={{0,96},{32,64},{64,32},{96,0},{1,97},{33,65},{65,33},{97,1},{2,98}... | collective-permute-start | bytes 480008 | tf_op jit(solution)/shard_map/ppermute | solution.py:281
  197.1 9.6 %copy-start.20 = (f32[50,800]{1,0:T(8,128)}, f32[50,800]{1,0:T(8,128)S(1)}, u32[]{:S(2)}) copy-start(f32[50,800]{1,0:T(8,128)S(1)} %collective-permute-done.15.refs_2_) | copy-start | bytes 480004
  197.1 2.7 %collective-permute-start.26 = (f32[20,800]{1,0:T(8,128)}, f32[20,800]{1,0:T(8,128)S(1)}, u32[]{:S(2)}, u32[]{:S(2)}) collective-permute-start(f32[20,800]{1,0:T(8,128)} %get-tuple-element.52), channel_id=1, source_target_pairs={{0,32},{32,0},{64,96},{96,64},{1,33},{33,1},{65,97},{97,65},{2,34}... | collective-permute-start | bytes 192008 | tf_op jit(solution)/shard_map/ppermute | solution.py:281
  197.2 9.5 %copy-start.21 = (f32[50,800]{1,0:T(8,128)}, f32[50,800]{1,0:T(8,128)S(1)}, u32[]{:S(2)}) copy-start(f32[50,800]{1,0:T(8,128)S(1)} %collective-permute-done.16.refs_3_) | copy-start | bytes 480004
  197.2 5.5 %collective-permute-start.27 = (f32[20,800]{1,0:T(8,128)}, f32[20,800]{1,0:T(8,128)S(1)}, u32[]{:S(2)}, u32[]{:S(2)}) collective-permute-start(f32[20,800]{1,0:T(8,128)} %get-tuple-element.53), channel_id=1, source_target_pairs={{0,64},{32,96},{64,0},{96,32},{1,65},{33,97},{65,1},{97,33},{2,66}... | collective-permute-start | bytes 192008 | tf_op jit(solution)/shard_map/ppermute | solution.py:281
  199.7 6.8 %collective-permute-start.28 = (f32[20,800]{1,0:T(8,128)}, f32[20,800]{1,0:T(8,128)S(1)}, u32[]{:S(2)}, u32[]{:S(2)}) collective-permute-start(f32[20,800]{1,0:T(8,128)} %get-tuple-element.54), channel_id=1, source_target_pairs={{0,96},{32,64},{64,32},{96,0},{1,97},{33,65},{65,33},{97,1},{2,98}... | collective-permute-start | bytes 192008 | tf_op jit(solution)/shard_map/ppermute | solution.py:281
  (11 other events, 26.1 us)
